TPU v7x, 32 devices: a whole 2x2x4 slice. The times are simulated.
32 devices in a mesh: gx: 4 (over z), gy: 8 (over y, x, core).
Axes of the slice: x: 2, y: 2, z: 4, core: 2. Of those that a mesh axis runs over, the one named last changes fastest.
Arguments:
- a_blocks: float32 [256, 4, 128, 128], P(('gx', 'gy')), may hold values from -0.25 to 0.25
- a_cols: int32 [256, 4], replicated, may hold values from 0 to 255, as said below
- t_blocks: float32 [256, 128, 128], P(('gx', 'gy')), may hold values from -0.5 to 0.5
- t_agg: int32 [256], replicated, may hold values from 0 to 1, as said below
- dinv: float32 [256, 128, 128], P(('gx', 'gy')), may hold values from -0.5 to 0.5
- coarse_inv: float32 [64, 128, 128], P(('gx', 'gy')), may hold values from -1.5 to 1.5
Outputs:
- coarse: float32 [64, 14, 128, 128], P(('gx', 'gy'))
Inputs may be any that keep to these rules, and one draw needn't show every extreme that they name: `a_cols`: block column 0 of row g is g itself; column 1 lies in g's own slab; column 2 lies in the slab below (on the cycle) and column 3 in the slab above; over the rows of one slab, columns 2 name exactly 4 distinct rows of the slab below, and columns 3 exactly 4 distinct rows of the slab above. `t_agg`: every slab's 2 aggregates each hold 4 of its rows.
All inputs are finite; a program needn't handle non-finite values.
Results may differ from a plain program's by a relative error of at most 0.0001.
Values sent between devices are 32-bit elements; how exact they have to be, the bound alone decides.
A program may use at most 64 MiB of HBM per device.

v0:
```python
import jax
import jax.numpy as jnp
from jax import lax
from jax.sharding import PartitionSpec as P

AGG_DEV = 2


OMEGA = 0.6


def shifted(value, axis, steps):
    count = lax.axis_size(axis)
    pairs = [(source, (source + steps) % count) for source in range(count)]
    return lax.ppermute(value, axis, pairs)


def read_list(a_cols, slab, side, rows):
    block_cols = lax.dynamic_slice_in_dim(a_cols, slab * rows, rows, 0)[:, 2 + side]
    offsets = block_cols % rows
    counter = jnp.arange(rows, dtype=jnp.int32)
    is_read = jnp.any(offsets[:, None] == counter[None, :], axis=0).astype(jnp.int32)
    ranks = jnp.cumsum(is_read) - 1
    width = rows // 2
    places = jnp.arange(width, dtype=jnp.int32)
    matched = (is_read[:, None] == 1) & (ranks[:, None] == places[None, :])
    return jnp.sum(jnp.where(matched, counter[:, None], 0), axis=0)


def place_rows(columns, lower_list, upper_list, device, devices, rows):
    slab = columns // rows
    offset = columns % rows
    lower_slab = (device + devices - 1) % devices
    width = lower_list.shape[0]
    counter = jnp.arange(width, dtype=jnp.int32)
    lower_pos = jnp.sum(jnp.where(lower_list == offset[..., None], counter, 0), axis=-1)
    upper_pos = (
        jnp.sum(jnp.where(upper_list == offset[..., None], counter, 0), axis=-1) + width + rows
    )
    own_pos = offset + width
    return jnp.where(slab == device, own_pos, jnp.where(slab == lower_slab, lower_pos, upper_pos))


def shards(a_blocks, a_cols, t_blocks, t_agg, dinv, coarse_inv):
    highest = lax.Precision.HIGHEST
    devices = lax.axis_size(("gx", "gy"))
    device = lax.axis_index(("gx", "gy"))
    rows = t_blocks.shape[0]
    previous = (device + devices - 1) % devices
    following = (device + 1) % devices
    labels = jnp.arange(a_cols.shape[0], dtype=jnp.int32) // rows * AGG_DEV + t_agg
    own_cols = lax.dynamic_slice_in_dim(a_cols, device * rows, rows, 0)
    lower_list = read_list(a_cols, device, 0, rows)
    upper_list = read_list(a_cols, device, 1, rows)
    places = place_rows(own_cols, lower_list, upper_list, device, devices, rows)
    to_upper = read_list(a_cols, following, 0, rows)
    to_lower = read_list(a_cols, previous, 1, rows)
    from_lower = shifted(t_blocks[to_upper], ("gx", "gy"), 1)
    from_upper = shifted(t_blocks[to_lower], ("gx", "gy"), -1)
    t_extended = jnp.concatenate([from_lower, t_blocks, from_upper], axis=0)
    t_cols = t_extended[places]
    prod_at = jnp.einsum("rkab,rkbc->rkac", a_blocks, t_cols, precision=highest)
    smoothed = jnp.einsum("rab,rkbc->rkac", dinv, prod_at, precision=highest)
    first = (jnp.arange(a_blocks.shape[1]) == 0).astype(jnp.float32)
    prolong = first[None, :, None, None] * t_blocks[:, None] - OMEGA * smoothed
    p_lower = shifted(prolong[to_upper], ("gx", "gy"), 1)
    p_upper = shifted(prolong[to_lower], ("gx", "gy"), -1)
    p_extended = jnp.concatenate([p_lower, prolong, p_upper], axis=0)
    near_labels = labels[own_cols]
    far_labels = labels[a_cols[own_cols]]
    columns_near = 5 * AGG_DEV
    column_ids = jnp.arange(columns_near, dtype=jnp.int32)
    block = t_blocks.shape[1]

    def accumulate(row, buffer):
        a_row = lax.dynamic_index_in_dim(a_blocks, row, 0, keepdims=False)
        gathered = p_extended[places[row]]
        partial_value = jnp.einsum("kab,kqbc->kqac", a_row, gathered, precision=highest)
        far = far_labels[row]
        far_column = (far // AGG_DEV - device + 2) % devices * AGG_DEV + far % AGG_DEV
        picker = (far_column[..., None] == column_ids).astype(jnp.float32)
        grouped = jnp.einsum("kqn,kqac->nac", picker, partial_value, precision=highest)
        p_row = lax.dynamic_index_in_dim(prolong, row, 0, keepdims=False)
        contrib = jnp.einsum("pba,nbc->pnac", p_row, grouped, precision=highest)
        near = near_labels[row]
        near_slab = (near // AGG_DEV - device + 1) % devices
        target = near_slab * AGG_DEV + near % AGG_DEV
        slot = ((column_ids // AGG_DEV)[None, :] - near_slab[:, None] + 2) * AGG_DEV + (
            column_ids % AGG_DEV
        )[None, :]
        target_all = jnp.broadcast_to(target[:, None], slot.shape)
        return buffer.at[target_all, slot].add(contrib)

    buffer = jnp.zeros((3 * AGG_DEV, 7 * AGG_DEV, block, block), jnp.float32)
    buffer = lax.fori_loop(0, rows, accumulate, buffer)
    from_next = shifted(buffer[:AGG_DEV], ("gx", "gy"), -1)
    from_prev = shifted(buffer[2 * AGG_DEV :], ("gx", "gy"), 1)
    galerkin = buffer[AGG_DEV : 2 * AGG_DEV] + from_next + from_prev
    return jnp.einsum("aij,asjk->asik", coarse_inv, galerkin, precision=highest)


def solution(mesh):
    placed = (
        P(("gx", "gy"), None, None, None),
        P(),
        P(("gx", "gy"), None, None),
        P(),
        P(("gx", "gy"), None, None),
        P(("gx", "gy"), None, None),
    )
    return jax.shard_map(
        shards,
        mesh=mesh,
        in_specs=placed,
        out_specs=P(("gx", "gy"), None, None, None),
        check_vma=False,
    )
```

profile of v0, /device:TPU:29, one launch (start us, length us, event | category | flops | bytes accessed | tf_op | source)
XLA Modules:
  0.0 308.5 jit_solution(14595781922891192059)
XLA Ops:
  9.2 3.5 %collective-permute-done.1 = f32[4,128,128]{2,1,0:T(8,128)} collective-permute-done((f32[4,128,128]{2,1,0:T(8,128)S(1)}, f32[4,128,128]{2,1,0:T(8,128)}, u32[]{:S(2)}, u32[]{:S(2)}) %collective-permute-start.1) | collective-permute-done | bytes 262176 | tf_op jit(solution)/shard_map/ppermute | solution.py:15
  15.8 5.7 %fusion.70 = f32[8,4,128,128]{3,2,1,0:T(8,128)S(1)} fusion(f32[8,4,128,128]{3,2,1,0:T(8,128)} %bitcast.155, f32[8,4,128,128]{3,2,1,0:T(8,128)} %param.8), kind=kOutput, calls=%fused_computation.174 | convolution fusion | flops 805306368 | bytes 6291456 | tf_op jit(solution)/shard_map/rkab,rkbc->rkac/dot_general | solution.py:62
  31.0 16.5 %collective-permute-done.2 = f32[4,4,128,128]{2,3,1,0:T(8,128)} collective-permute-done((f32[4,4,128,128]{2,3,1,0:T(8,128)}, f32[4,4,128,128]{2,3,1,0:T(8,128)}, u32[]{:S(2)}, u32[]{:S(2)}) %collective-permute-start.2) | collective-permute-done | bytes 1048608 | tf_op jit(solution)/shard_map/ppermute | solution.py:15
  47.5 6.0 %collective-permute-done.3 = f32[4,4,128,128]{2,3,1,0:T(8,128)} collective-permute-done((f32[4,4,128,128]{2,3,1,0:T(8,128)}, f32[4,4,128,128]{2,3,1,0:T(8,128)}, u32[]{:S(2)}, u32[]{:S(2)}) %collective-permute-start.3) | collective-permute-done | bytes 1048608 | tf_op jit(solution)/shard_map/ppermute | solution.py:15
  53.5 3.9 %pad_maximum_fusion = f32[16,4,128,128]{2,3,1,0:T(8,128)} fusion(f32[4,4,128,128]{2,3,1,0:T(8,128)} %collective-permute-done.3, f32[8,4,128,128]{2,3,1,0:T(8,128)S(1)} %bitcast_subtract_fusion, f32[4,4,128,128]{2,3,1,0:T(8,128)} %collective-permute-done.2), kind=kLoop, calls=%fused_computation.76 | loop fusion | flops 2097152 | bytes 8388608 | tf_op jit(solution)/shard_map/concatenate | solution.py:68
  57.4 5.4 %copy.42 = f32[16,4,128,128]{3,2,1,0:T(8,128)} copy(f32[16,4,128,128]{2,3,1,0:T(8,128)} %pad_maximum_fusion) | data formatting | bytes 8388608
  62.8 3.1 broadcast_in_dim.132
  65.9 193.3 %while.19 = (s32[]{:T(128)}, f32[6,14,128,128]{3,2,1,0:T(8,128)}, s32[8,4]{1,0:T(8,128)S(1)}, s32[]{:T(128)}, s32[8,4,4]{2,1,0:T(4,128)S(1)}, /*index=5*/s32[8,4...) while((s32[]{:T(128)}, f32[6,14,128,128]{3,2,1,0:T(8,128)}, ...), condition=%wide.region_16.17_spmd.clone.clone, body=%wide.region_14.16_spmd.clone.clone.sunk | while | flops 1441401472 | bytes 41686536 | solution.py:95
  67.3 2.8 gather_fusion
  74.4 3.2 %convolution_bitcast_fusion.8 = f32[4,10,128,128]{2,3,0,1:T(8,128)S(1)} fusion(f32[10,128,128,1]{2,0,1,3:T(8,128)S(1)} %convolution_bitcast_fusion.7, f32[8,4,128,128]{2,3,1,0:T(8,128)} %copy-done.1, s32[]{:T(128)S(6)} %copy.69), kind=kOutput, calls=%fused_computation.14.clone.1 | convolution fusion | flops 1006632960 | bytes 3538948 | tf_op jit(solution)/shard_map/while/body/eval_jaxpr/pba,nbc->pnac/dot_general | solution.py:84
  79.7 10.4 %scatter_fusion = f32[6,14,128,128]{3,2,1,0:T(8,128)} fusion(f32[6,14,128,128]{3,2,1,0:T(8,128)} %get-tuple-element.569, s32[40]{0:T(128)S(1)} %reshape.694, f32[40,128,128]{2,1,0:T(8,128)} %bitcast.154), kind=kCustom, calls=%fused_computation.9.clone.clone.1 | custom fusion | flops 655360 | bytes 7864640 | tf_op jit(solution)/shard_map/while/body/eval_jaxpr/scatter-add | solution.py:92
  91.5 2.8 gather_fusion
  98.6 3.2 %convolution_bitcast_fusion.8 = f32[4,10,128,128]{2,3,0,1:T(8,128)S(1)} fusion(f32[10,128,128,1]{2,0,1,3:T(8,128)S(1)} %convolution_bitcast_fusion.7, f32[8,4,128,128]{2,3,1,0:T(8,128)} %copy-done.1, s32[]{:T(128)S(6)} %copy.69), kind=kOutput, calls=%fused_computation.14.clone.1 | convolution fusion | flops 1006632960 | bytes 3538948 | tf_op jit(solution)/shard_map/while/body/eval_jaxpr/pba,nbc->pnac/dot_general | solution.py:84
  103.9 10.4 %scatter_fusion = f32[6,14,128,128]{3,2,1,0:T(8,128)} fusion(f32[6,14,128,128]{3,2,1,0:T(8,128)} %get-tuple-element.569, s32[40]{0:T(128)S(1)} %reshape.694, f32[40,128,128]{2,1,0:T(8,128)} %bitcast.154), kind=kCustom, calls=%fused_computation.9.clone.clone.1 | custom fusion | flops 655360 | bytes 7864640 | tf_op jit(solution)/shard_map/while/body/eval_jaxpr/scatter-add | solution.py:92
  122.8 3.2 %convolution_bitcast_fusion.8 = f32[4,10,128,128]{2,3,0,1:T(8,128)S(1)} fusion(f32[10,128,128,1]{2,0,1,3:T(8,128)S(1)} %convolution_bitcast_fusion.7, f32[8,4,128,128]{2,3,1,0:T(8,128)} %copy-done.1, s32[]{:T(128)S(6)} %copy.69), kind=kOutput, calls=%fused_computation.14.clone.1 | convolution fusion | flops 1006632960 | bytes 3538948 | tf_op jit(solution)/shard_map/while/body/eval_jaxpr/pba,nbc->pnac/dot_general | solution.py:84
  128.1 10.4 %scatter_fusion = f32[6,14,128,128]{3,2,1,0:T(8,128)} fusion(f32[6,14,128,128]{3,2,1,0:T(8,128)} %get-tuple-element.569, s32[40]{0:T(128)S(1)} %reshape.694, f32[40,128,128]{2,1,0:T(8,128)} %bitcast.154), kind=kCustom, calls=%fused_computation.9.clone.clone.1 | custom fusion | flops 655360 | bytes 7864640 | tf_op jit(solution)/shard_map/while/body/eval_jaxpr/scatter-add | solution.py:92
  139.9 2.8 gather_fusion
  147.0 3.2 %convolution_bitcast_fusion.8 = f32[4,10,128,128]{2,3,0,1:T(8,128)S(1)} fusion(f32[10,128,128,1]{2,0,1,3:T(8,128)S(1)} %convolution_bitcast_fusion.7, f32[8,4,128,128]{2,3,1,0:T(8,128)} %copy-done.1, s32[]{:T(128)S(6)} %copy.69), kind=kOutput, calls=%fused_computation.14.clone.1 | convolution fusion | flops 1006632960 | bytes 3538948 | tf_op jit(solution)/shard_map/while/body/eval_jaxpr/pba,nbc->pnac/dot_general | solution.py:84
  152.3 10.4 %scatter_fusion = f32[6,14,128,128]{3,2,1,0:T(8,128)} fusion(f32[6,14,128,128]{3,2,1,0:T(8,128)} %get-tuple-element.569, s32[40]{0:T(128)S(1)} %reshape.694, f32[40,128,128]{2,1,0:T(8,128)} %bitcast.154), kind=kCustom, calls=%fused_computation.9.clone.clone.1 | custom fusion | flops 655360 | bytes 7864640 | tf_op jit(solution)/shard_map/while/body/eval_jaxpr/scatter-add | solution.py:92
  171.1 3.2 %convolution_bitcast_fusion.8 = f32[4,10,128,128]{2,3,0,1:T(8,128)S(1)} fusion(f32[10,128,128,1]{2,0,1,3:T(8,128)S(1)} %convolution_bitcast_fusion.7, f32[8,4,128,128]{2,3,1,0:T(8,128)} %copy-done.1, s32[]{:T(128)S(6)} %copy.69), kind=kOutput, calls=%fused_computation.14.clone.1 | convolution fusion | flops 1006632960 | bytes 3538948 | tf_op jit(solution)/shard_map/while/body/eval_jaxpr/pba,nbc->pnac/dot_general | solution.py:84
  176.5 10.4 %scatter_fusion = f32[6,14,128,128]{3,2,1,0:T(8,128)} fusion(f32[6,14,128,128]{3,2,1,0:T(8,128)} %get-tuple-element.569, s32[40]{0:T(128)S(1)} %reshape.694, f32[40,128,128]{2,1,0:T(8,128)} %bitcast.154), kind=kCustom, calls=%fused_computation.9.clone.clone.1 | custom fusion | flops 655360 | bytes 7864640 | tf_op jit(solution)/shard_map/while/body/eval_jaxpr/scatter-add | solution.py:92
  188.2 2.8 gather_fusion
  195.3 3.2 %convolution_bitcast_fusion.8 = f32[4,10,128,128]{2,3,0,1:T(8,128)S(1)} fusion(f32[10,128,128,1]{2,0,1,3:T(8,128)S(1)} %convolution_bitcast_fusion.7, f32[8,4,128,128]{2,3,1,0:T(8,128)} %copy-done.1, s32[]{:T(128)S(6)} %copy.69), kind=kOutput, calls=%fused_computation.14.clone.1 | convolution fusion | flops 1006632960 | bytes 3538948 | tf_op jit(solution)/shard_map/while/body/eval_jaxpr/pba,nbc->pnac/dot_general | solution.py:84
  200.6 10.4 %scatter_fusion = f32[6,14,128,128]{3,2,1,0:T(8,128)} fusion(f32[6,14,128,128]{3,2,1,0:T(8,128)} %get-tuple-element.569, s32[40]{0:T(128)S(1)} %reshape.694, f32[40,128,128]{2,1,0:T(8,128)} %bitcast.154), kind=kCustom, calls=%fused_computation.9.clone.clone.1 | custom fusion | flops 655360 | bytes 7864640 | tf_op jit(solution)/shard_map/while/body/eval_jaxpr/scatter-add | solution.py:92
  212.4 2.8 gather_fusion
  219.5 3.2 %convolution_bitcast_fusion.8 = f32[4,10,128,128]{2,3,0,1:T(8,128)S(1)} fusion(f32[10,128,128,1]{2,0,1,3:T(8,128)S(1)} %convolution_bitcast_fusion.7, f32[8,4,128,128]{2,3,1,0:T(8,128)} %copy-done.1, s32[]{:T(128)S(6)} %copy.69), kind=kOutput, calls=%fused_computation.14.clone.1 | convolution fusion | flops 1006632960 | bytes 3538948 | tf_op jit(solution)/shard_map/while/body/eval_jaxpr/pba,nbc->pnac/dot_general | solution.py:84
  224.8 10.3 %scatter_fusion = f32[6,14,128,128]{3,2,1,0:T(8,128)} fusion(f32[6,14,128,128]{3,2,1,0:T(8,128)} %get-tuple-element.569, s32[40]{0:T(128)S(1)} %reshape.694, f32[40,128,128]{2,1,0:T(8,128)} %bitcast.154), kind=kCustom, calls=%fused_computation.9.clone.clone.1 | custom fusion | flops 655360 | bytes 7864640 | tf_op jit(solution)/shard_map/while/body/eval_jaxpr/scatter-add | solution.py:92
  236.5 2.8 gather_fusion
  243.6 3.2 %convolution_bitcast_fusion.8 = f32[4,10,128,128]{2,3,0,1:T(8,128)S(1)} fusion(f32[10,128,128,1]{2,0,1,3:T(8,128)S(1)} %convolution_bitcast_fusion.7, f32[8,4,128,128]{2,3,1,0:T(8,128)} %copy-done.1, s32[]{:T(128)S(6)} %copy.69), kind=kOutput, calls=%fused_computation.14.clone.1 | convolution fusion | flops 1006632960 | bytes 3538948 | tf_op jit(solution)/shard_map/while/body/eval_jaxpr/pba,nbc->pnac/dot_general | solution.py:84
  248.9 10.3 %scatter_fusion = f32[6,14,128,128]{3,2,1,0:T(8,128)} fusion(f32[6,14,128,128]{3,2,1,0:T(8,128)} %get-tuple-element.569, s32[40]{0:T(128)S(1)} %reshape.694, f32[40,128,128]{2,1,0:T(8,128)} %bitcast.154), kind=kCustom, calls=%fused_computation.9.clone.clone.1 | custom fusion | flops 655360 | bytes 7864640 | tf_op jit(solution)/shard_map/while/body/eval_jaxpr/scatter-add | solution.py:92
  263.5 38.7 %collective-permute-done.4 = f32[2,14,128,128]{3,2,1,0:T(8,128)S(1)} collective-permute-done((f32[2,14,128,128]{3,2,1,0:T(8,128)S(1)}, f32[2,14,128,128]{3,2,1,0:T(8,128)S(1)}, u32[]{:S(2)}, u32[]{:S(2)}) %collective-permute-start.4) | collective-permute-done | bytes 1835040 | tf_op jit(solution)/shard_map/ppermute | solution.py:15
  302.2 4.6 %fusion.42 = f32[2,14,128,128]{2,3,1,0:T(8,128)S(1)} fusion(f32[2,14,128,128]{3,2,1,0:T(8,128)S(1)} %collective-permute-done.5, f32[2,14,128,128]{3,2,1,0:T(8,128)S(1)} %collective-permute-done.4, f32[6,14,128,128]{3,2,1,0:T(8,128)} %get-tuple-element.366, f32[2,128,128]{2,1,0:T(8,128)S(1)} %copy-done.4), kind=kOutput, calls=%fused_computation.84 | convolution fusion | flops 705560576 | bytes 7471104 | tf_op jit(solution)/shard_map/aij,asjk->asik/dot_general | solution.py:99
  (207 shorter events, 94.8 us)
Async XLA Ops:
  0.0 21.5 %copy-start = (f32[8,128,128]{2,1,0:T(8,128)S(1)}, f32[8,128,128]{2,1,0:T(8,128)}, u32[]{:S(2)}) copy-start(f32[8,128,128]{2,1,0:T(8,128)} %param.12) | copy-start | bytes 1572868
  0.0 12.8 %copy-start.3 = (f32[8,128,128]{2,1,0:T(8,128)S(1)}, f32[8,128,128]{2,1,0:T(8,128)}, u32[]{:S(2)}) copy-start(f32[8,128,128]{2,1,0:T(8,128)} %param.10) | copy-start | bytes 1572868
  2.9 6.3 %collective-permute-start = (f32[4,128,128]{2,1,0:T(8,128)S(1)}, f32[4,128,128]{2,1,0:T(8,128)S(1)}, u32[]{:S(2)}, u32[]{:S(2)}) collective-permute-start(f32[4,128,128]{2,1,0:T(8,128)S(1)} %gather_fusion.4), channel_id=1, source_target_pairs={{0,1},{1,2},{2,3},{3,4},{4,5},{5,6},{6,7},{7,8},{8,9},{9,10},{10,1... | collective-permute-start | bytes 786440 | tf_op jit(solution)/shard_map/ppermute | solution.py:15
  6.8 6.0 %collective-permute-start.1 = (f32[4,128,128]{2,1,0:T(8,128)S(1)}, f32[4,128,128]{2,1,0:T(8,128)}, u32[]{:S(2)}, u32[]{:S(2)}) collective-permute-start(f32[4,128,128]{2,1,0:T(8,128)S(1)} %gather_fusion.5), channel_id=1, source_target_pairs={{0,31},{1,0},{2,1},{3,2},{4,3},{5,4},{6,5},{7,6},{8,7},{9,8},{10,9... | collective-permute-start | bytes 786440 | tf_op jit(solution)/shard_map/ppermute | solution.py:15
  23.7 3.7 %copy-start.5 = (s32[256,4]{0,1:T(4,128)S(1)}, s32[256,4]{0,1:T(4,128)}, u32[]{:S(2)}) copy-start(s32[256,4]{0,1:T(4,128)} %param.9) | copy-start | bytes 12292
  23.7 4.1 %copy-start.6 = (s32[256]{0:T(256)S(1)}, s32[256]{0:T(256)}, u32[]{:S(2)}) copy-start(s32[256]{0:T(256)} %param.11) | copy-start | bytes 3076
  26.9 20.6 %collective-permute-start.2 = (f32[4,4,128,128]{2,3,1,0:T(8,128)}, f32[4,4,128,128]{2,3,1,0:T(8,128)}, u32[]{:S(2)}, u32[]{:S(2)}) collective-permute-start(f32[4,4,128,128]{2,3,1,0:T(8,128)} %gather_fusion.7), channel_id=1, source_target_pairs={{0,1},{1,2},{2,3},{3,4},{4,5},{5,6},{6,7},{7,8},{8,9},{9,10},{10,1... | collective-permute-start | bytes 3145736 | tf_op jit(solution)/shard_map/ppermute | solution.py:15
  26.9 26.6 %collective-permute-start.3 = (f32[4,4,128,128]{2,3,1,0:T(8,128)}, f32[4,4,128,128]{2,3,1,0:T(8,128)}, u32[]{:S(2)}, u32[]{:S(2)}) collective-permute-start(f32[4,4,128,128]{2,3,1,0:T(8,128)} %gather_fusion.8), channel_id=1, source_target_pairs={{0,31},{1,0},{2,1},{3,2},{4,3},{5,4},{6,5},{7,6},{8,7},{9,8},{10,9... | collective-permute-start | bytes 3145736 | tf_op jit(solution)/shard_map/ppermute | solution.py:15
  65.9 1.4 copy-start.1
  79.7 10.4 %copy-start.2 = (f32[8,4,128,128]{2,3,1,0:T(8,128)S(1)}, f32[8,4,128,128]{2,3,1,0:T(8,128)}, u32[]{:S(2)}) copy-start(f32[8,4,128,128]{2,3,1,0:T(8,128)} %copy-done.1) | copy-start | bytes 6291460 | tf_op jit(solution)/shard_map/while
  90.1 1.4 copy-start.1
  103.9 10.4 %copy-start.2 = (f32[8,4,128,128]{2,3,1,0:T(8,128)S(1)}, f32[8,4,128,128]{2,3,1,0:T(8,128)}, u32[]{:S(2)}) copy-start(f32[8,4,128,128]{2,3,1,0:T(8,128)} %copy-done.1) | copy-start | bytes 6291460 | tf_op jit(solution)/shard_map/while
  114.3 1.4 copy-start.1
  128.1 10.4 %copy-start.2 = (f32[8,4,128,128]{2,3,1,0:T(8,128)S(1)}, f32[8,4,128,128]{2,3,1,0:T(8,128)}, u32[]{:S(2)}) copy-start(f32[8,4,128,128]{2,3,1,0:T(8,128)} %copy-done.1) | copy-start | bytes 6291460 | tf_op jit(solution)/shard_map/while
  138.5 1.4 copy-start.1
  152.3 10.4 %copy-start.2 = (f32[8,4,128,128]{2,3,1,0:T(8,128)S(1)}, f32[8,4,128,128]{2,3,1,0:T(8,128)}, u32[]{:S(2)}) copy-start(f32[8,4,128,128]{2,3,1,0:T(8,128)} %copy-done.1) | copy-start | bytes 6291460 | tf_op jit(solution)/shard_map/while
  162.7 1.4 copy-start.1
  176.5 10.4 %copy-start.2 = (f32[8,4,128,128]{2,3,1,0:T(8,128)S(1)}, f32[8,4,128,128]{2,3,1,0:T(8,128)}, u32[]{:S(2)}) copy-start(f32[8,4,128,128]{2,3,1,0:T(8,128)} %copy-done.1) | copy-start | bytes 6291460 | tf_op jit(solution)/shard_map/while
  186.9 1.4 copy-start.1
  200.6 10.4 %copy-start.2 = (f32[8,4,128,128]{2,3,1,0:T(8,128)S(1)}, f32[8,4,128,128]{2,3,1,0:T(8,128)}, u32[]{:S(2)}) copy-start(f32[8,4,128,128]{2,3,1,0:T(8,128)} %copy-done.1) | copy-start | bytes 6291460 | tf_op jit(solution)/shard_map/while
  211.0 1.4 copy-start.1
  224.8 10.3 %copy-start.2 = (f32[8,4,128,128]{2,3,1,0:T(8,128)S(1)}, f32[8,4,128,128]{2,3,1,0:T(8,128)}, u32[]{:S(2)}) copy-start(f32[8,4,128,128]{2,3,1,0:T(8,128)} %copy-done.1) | copy-start | bytes 6291460 | tf_op jit(solution)/shard_map/while
  235.1 1.4 copy-start.1
  248.9 10.3 %copy-start.2 = (f32[8,4,128,128]{2,3,1,0:T(8,128)S(1)}, f32[8,4,128,128]{2,3,1,0:T(8,128)}, u32[]{:S(2)}) copy-start(f32[8,4,128,128]{2,3,1,0:T(8,128)} %copy-done.1) | copy-start | bytes 6291460 | tf_op jit(solution)/shard_map/while
  259.2 43.0 %copy-start.4 = (f32[2,128,128]{2,1,0:T(8,128)S(1)}, f32[2,128,128]{2,1,0:T(8,128)}, u32[]{:S(2)}) copy-start(f32[2,128,128]{2,1,0:T(8,128)} %param.13) | copy-start | bytes 393220
  261.7 40.5 %collective-permute-start.4 = (f32[2,14,128,128]{3,2,1,0:T(8,128)S(1)}, f32[2,14,128,128]{3,2,1,0:T(8,128)S(1)}, u32[]{:S(2)}, u32[]{:S(2)}) collective-permute-start(f32[2,14,128,128]{3,2,1,0:T(8,128)S(1)} %get-tuple-element.477), channel_id=1, source_target_pairs={{0,31},{1,0},{2,1},{3,2},{4,3},{5,4},{6,5},{7,6},{8,7},{9,8},{10,9... | collective-permute-start | bytes 5505032 | tf_op jit(solution)/shard_map/ppermute | solution.py:15
  261.8 40.4 %collective-permute-start.5 = (f32[2,14,128,128]{3,2,1,0:T(8,128)S(1)}, f32[2,14,128,128]{3,2,1,0:T(8,128)S(1)}, u32[]{:S(2)}, u32[]{:S(2)}) collective-permute-start(f32[2,14,128,128]{3,2,1,0:T(8,128)S(1)} %get-tuple-element.478), channel_id=1, source_target_pairs={{0,1},{1,2},{2,3},{3,4},{4,5},{5,6},{6,7},{7,8},{8,9},{9,10},{10,1... | collective-permute-start | bytes 5505032 | tf_op jit(solution)/shard_map/ppermute | solution.py:15
where the time goes:
time: 313 us; the launch traced here: 309 us
  other arithmetic  91.8 us (29%)
  local copies, waits for them, and re-layouts  79.2 us (25%)
  matrix products  67.9 us (22%)
  waiting for transfers between devices  64.7 us (21%)
  starting transfers between devices  4.19 us (1%)
    scatter-add x8, other arithmetic, accumulate(): return buffer.at[target_all, slot].add(contrib)  83 us
    ppermute x6, waiting for transfers between devices, shifted(): return lax.ppermute(value, axis, pairs)  64.7 us
    dot_general x8, matrix products, accumulate(): contrib = jnp.einsum('pba,nbc->pnac', p_row, grouped, precision=highest)  25.9 us
    gather x8, local copies, waits for them, and re-layouts, accumulate(): gathered = p_extended[places[row]]  22.4 us
    dot_general x8, matrix products, accumulate(): jnp.einsum('kab,kqbc->kqac', a_row, gathered, precision=highest)  22.2 us
    transpose x8, local copies, waits for them, and re-layouts, accumulate(): contrib = jnp.einsum('pba,nbc->pnac', p_row, grouped, precision=highest)  16.6 us
    while x32, local copies, waits for them, and re-layouts  8.93 us
    dot_general x8, matrix products, accumulate(): jnp.einsum('kqn,kqac->nac', picker, partial_value, precision=highest)  7.41 us
  transfers between devices with their start and end apart: 6, of which 4 were waited for; matrix products, arithmetic and copies ran while one was open for 3% of the time, Pallas kernels for 0%

commit v1 on v0

v1 whole, which is shorter than its diff:
```python
import functools

import jax
import jax.numpy as jnp
from jax import lax
from jax.experimental import pallas as pl
from jax.experimental.pallas import tpu as pltpu
from jax.sharding import PartitionSpec as P

AGG_DEV = 2

OMEGA = 0.6

F32 = jnp.float32
BF16 = jnp.bfloat16
MESH = pl.DeviceIdType.MESH

SEND_ORDER = (1, 3, 2, 0, 4)
FINAL_ORDER = (1, 5, 3, 2, 0, 4, 6)


def read_list(a_cols, slab, side, rows):
    block_cols = lax.dynamic_slice_in_dim(a_cols, slab * rows, rows, 0)[:, 2 + side]
    offsets = block_cols % rows
    counter = jnp.arange(rows, dtype=jnp.int32)
    is_read = jnp.any(offsets[:, None] == counter[None, :], axis=0).astype(jnp.int32)
    ranks = jnp.sum(jnp.where(counter[None, :] < counter[:, None], is_read[None, :], 0), axis=1)
    places = jnp.arange(rows // 2, dtype=jnp.int32)
    matched = (is_read[:, None] == 1) & (ranks[:, None] == places[None, :])
    return jnp.sum(jnp.where(matched, counter[:, None], 0), axis=0)


def indices(a_cols, t_agg, device, devices, rows):
    previous = (device + devices - 1) % devices
    following = (device + 1) % devices
    own = lax.dynamic_slice_in_dim(a_cols, device * rows, rows, 0)
    offsets = own % rows
    lower_list = read_list(a_cols, device, 0, rows)
    upper_list = read_list(a_cols, device, 1, rows)
    to_upper = read_list(a_cols, following, 0, rows)
    to_lower = read_list(a_cols, previous, 1, rows)
    places = jnp.arange(rows // 2, dtype=jnp.int32)

    def rank(entries, offs):
        return jnp.sum(jnp.where(entries[None, :] == offs[:, None], places[None, :], 0), axis=1)

    labels = t_agg[own]
    low_cols = a_cols[previous * rows + lower_list][:, 2:4]
    up_cols = a_cols[following * rows + upper_list][:, 2:4]
    low_labels = t_agg[low_cols]
    up_labels = t_agg[up_cols]
    return jnp.concatenate(
        [
            offsets[:, 1],
            rank(lower_list, offsets[:, 2]),
            rank(upper_list, offsets[:, 3]),
            labels.T.reshape(-1),
            to_upper,
            to_lower,
            low_labels.T.reshape(-1),
            up_labels.T.reshape(-1),
        ]
    ).astype(jnp.int32)


def split(x):
    high = x.astype(BF16)
    return high, (x - high.astype(F32)).astype(BF16)


def dot3(ah, al, bh, bl):
    def dot(x, y):
        return jnp.dot(x, y, preferred_element_type=F32)

    return dot(ah, bh) + (dot(ah, bl) + dot(al, bh))


def kernel(
    rows, gx_size, gy_size,
    idx, a_hbm, t_hbm, d_hbm, c_hbm, out,
    a_v, t_v, d_v, c_v,
    ah, al, bh, bl, th, tl,
    t_send, t_recv, own_c, far_c, po_send, po_recv, pf_send, pf_recv,
    pdh, pdl, ndh, ndl, pth, ptl, aph, apl,
    g_send, g_recv, g_own,
    load_sem, send_sem, recv_sem,
):
    fetch = rows // 2
    blk = t_v.shape[-1]
    wide = AGG_DEV * blk
    devices = gx_size * gy_size
    me = lax.axis_index("gx") * gy_size + lax.axis_index("gy")
    following = lax.rem(me + 1, devices)
    previous = lax.rem(me + devices - 1, devices)

    def place(d):
        return (d // gy_size, lax.rem(d, gy_size))

    targets = (place(following), place(previous))

    barrier = pltpu.get_barrier_semaphore()
    for target in targets:
        pl.semaphore_signal(barrier, inc=1, device_id=target, device_id_type=MESH)

    loads = []
    for n, (src, dst) in enumerate(((t_hbm, t_v), (d_hbm, d_v), (a_hbm, a_v), (c_hbm, c_v))):
        copy = pltpu.make_async_copy(src, dst, load_sem.at[n])
        copy.start()
        loads.append(copy)

    def send(src, dst, side, n):
        copy = pltpu.make_async_remote_copy(
            src_ref=src,
            dst_ref=dst,
            send_sem=send_sem.at[side, n],
            recv_sem=recv_sem.at[side, n],
            device_id=targets[side],
            device_id_type=MESH,
        )
        copy.start()
        return copy

    base_c1, base_lp, base_up = 0, rows, 2 * rows
    base_lab = 3 * rows
    base_to = 7 * rows
    base_near = base_to + 2 * fetch

    loads[0].wait()
    for side in range(2):
        for j in range(fetch):
            t_send[side, j] = t_v[idx[base_to + side * fetch + j]]
    pl.semaphore_wait(barrier, 2)
    t_copies = [send(t_send.at[side], t_recv.at[side], side, 0) for side in range(2)]

    loads[1].wait()
    loads[2].wait()

    @pl.loop(0, rows)
    def _(g):
        h, l = split(t_v[g])
        th[g], tl[g] = h, l
        dh, dl = split(d_v[g])
        for k in range(4):
            h, l = split(a_v[g, k])
            ah[g, :, k * blk:(k + 1) * blk] = h
            al[g, :, k * blk:(k + 1) * blk] = l
        h, l = split(-OMEGA * dot3(dh, dl, ah[g], al[g]))
        bh[g], bl[g] = h, l

    def mask(position, value):
        return (idx[position] == value).astype(F32)

    @pl.loop(0, rows)
    def _(g):
        c1 = idx[base_c1 + g]
        p0 = t_v[g] + dot3(bh[g, :, 0:blk], bl[g, :, 0:blk], th[g], tl[g])
        p1 = dot3(bh[g, :, blk:2 * blk], bl[g, :, blk:2 * blk], th[c1], tl[c1])
        for v in range(AGG_DEV):
            own_c[g, :, v * blk:(v + 1) * blk] = p0 * mask(base_lab + g, v) + p1 * mask(base_lab + rows + g, v)

    for side in range(2):
        for j in range(fetch):
            po_send[side, j] = own_c[idx[base_to + side * fetch + j]]
    po_copies = [send(po_send.at[side], po_recv.at[side], side, 1) for side in range(2)]

    for copy in t_copies:
        copy.wait_recv()

    for side in range(2):
        for j in range(fetch):
            h, l = split(t_recv[side, j])
            th[rows + side * fetch + j] = h
            tl[rows + side * fetch + j] = l

    @pl.loop(0, rows)
    def _(g):
        for side in range(2):
            at = rows + side * fetch + idx[(base_lp, base_up)[side] + g]
            cols = slice((2 + side) * blk, (3 + side) * blk)
            far_c[g, :, side * blk:(side + 1) * blk] = dot3(bh[g, :, cols], bl[g, :, cols], th[at], tl[at])

    for side in range(2):
        for j in range(fetch):
            pf_send[side, j] = far_c[idx[base_to + side * fetch + j]]
    pf_copies = [send(pf_send.at[side], pf_recv.at[side], side, 2) for side in range(2)]

    @pl.loop(0, rows)
    def _(g):
        at = pl.ds(pl.multiple_of(g * blk, blk), blk)
        h, l = split(own_c[g])
        pdh[g, 1], pdl[g, 1] = h, l
        for v in range(AGG_DEV):
            cols = slice(v * blk, (v + 1) * blk)
            h, l = split(own_c[g, :, cols].T)
            pth[1, cols, at] = h
            ptl[1, cols, at] = l
        for side in range(2):
            block = far_c[g, :, side * blk:(side + 1) * blk]
            flip = block.T
            for v in range(AGG_DEV):
                cols = slice(v * blk, (v + 1) * blk)
                keep = mask(base_lab + (2 + side) * rows + g, v)
                h, l = split(block * keep)
                pdh[g, 2 * side, :, cols] = h
                pdl[g, 2 * side, :, cols] = l
                h, l = split(flip * keep)
                pth[2 * side, cols, at] = h
                ptl[2 * side, cols, at] = l

    for copy in po_copies:
        copy.wait_recv()
    for side in range(2):
        for j in range(fetch):
            h, l = split(po_recv[side, j])
            ndh[side * fetch + j, 1] = h
            ndl[side * fetch + j, 1] = l

    def product(n):
        @pl.loop(0, rows)
        def _(g):
            c1 = idx[base_c1 + g]
            lp = idx[base_lp + g]
            up = fetch + idx[base_up + g]
            tops, bottoms = [], []
            parts = []
            if 1 <= n <= 3:
                parts += [(0, pdh, pdl, g, n - 1), (1, pdh, pdl, c1, n - 1)]
            if n <= 2:
                parts += [(2, ndh, ndl, lp, n)]
            if n >= 2:
                parts += [(3, ndh, ndl, up, n - 2)]
            for _, high, low, row, at in parts:
                tops.append(high[row, at])
                bottoms.append(low[row, at])
            slots = [p[0] for p in parts]
            if slots == list(range(slots[0], slots[0] + len(slots))):
                xh = ah[g, :, slots[0] * blk:(slots[-1] + 1) * blk]
                xl = al[g, :, slots[0] * blk:(slots[-1] + 1) * blk]
            else:
                xh = jnp.concatenate([ah[g, :, k * blk:(k + 1) * blk] for k in slots], axis=1)
                xl = jnp.concatenate([al[g, :, k * blk:(k + 1) * blk] for k in slots], axis=1)
            yh = jnp.concatenate(tops, axis=0) if len(tops) > 1 else tops[0]
            yl = jnp.concatenate(bottoms, axis=0) if len(bottoms) > 1 else bottoms[0]
            h, l = split(dot3(xh, xl, yh, yl))
            at = pl.ds(pl.multiple_of(g * blk, blk), blk)
            aph[n, at, :] = h
            apl[n, at, :] = l

    g_copies = {}

    def neighbours(n):
        for side in range(2):
            r = 2 - 2 * side
            g_send[side, n] = dot3(pth[r], ptl[r], aph[n], apl[n])
            g_copies[side, n] = send(g_send.at[side, n], g_recv.at[side, n], side, 3 + n)

    for n in SEND_ORDER[:2]:
        product(n)
        neighbours(n)

    for copy in pf_copies:
        copy.wait_recv()

    @pl.loop(0, fetch)
    def _(j):
        for owner in range(2):
            for side in range(2):
                block = pf_recv[owner, j, :, side * blk:(side + 1) * blk]
                for v in range(AGG_DEV):
                    keep = mask(base_near + (owner * 2 + side) * fetch + j, v)
                    h, l = split(block * keep)
                    cols = slice(v * blk, (v + 1) * blk)
                    ndh[owner * fetch + j, 2 * side, :, cols] = h
                    ndl[owner * fetch + j, 2 * side, :, cols] = l

    for n in SEND_ORDER[2:]:
        product(n)
        neighbours(n)

    for n in SEND_ORDER:
        g_own[n] = dot3(pth[1], ptl[1], aph[n], apl[n])

    loads[3].wait()
    inverses = [split(c_v[a]) for a in range(AGG_DEV)]
    for j in FINAL_ORDER:
        if j <= 4:
            g_copies[0, j].wait_recv()
        if j >= 2:
            g_copies[1, j - 2].wait_recv()
        for a in range(AGG_DEV):
            at = slice(a * blk, (a + 1) * blk)
            terms = []
            if 1 <= j <= 5:
                terms.append(g_own[j - 1, at, :])
            if j <= 4:
                terms.append(g_recv[0, j, at, :])
            if j >= 2:
                terms.append(g_recv[1, j - 2, at, :])
            h, l = split(functools.reduce(jnp.add, terms))
            result = dot3(inverses[a][0], inverses[a][1], h, l)
            for v in range(AGG_DEV):
                out[a, AGG_DEV * j + v] = result[:, v * blk:(v + 1) * blk]

    for copy in [*t_copies, *po_copies, *pf_copies, *g_copies.values()]:
        copy.wait_send()


def shards(gx_size, gy_size, a_blocks, a_cols, t_blocks, t_agg, dinv, coarse_inv):
    devices = gx_size * gy_size
    device = lax.axis_index(("gx", "gy"))
    rows, blk = t_blocks.shape[0], t_blocks.shape[1]
    fetch = rows // 2
    wide = AGG_DEV * blk
    idx = indices(a_cols, t_agg, device, devices, rows)
    hbm = pl.BlockSpec(memory_space=pl.ANY)
    scratch = [
        pltpu.VMEM(a_blocks.shape, F32),
        pltpu.VMEM(t_blocks.shape, F32),
        pltpu.VMEM(dinv.shape, F32),
        pltpu.VMEM(coarse_inv.shape, F32),
        *[pltpu.VMEM((rows, blk, 4 * blk), BF16)] * 4,
        *[pltpu.VMEM((rows + 2 * fetch, blk, blk), BF16)] * 2,
        *[pltpu.VMEM((2, fetch, blk, blk), F32)] * 2,
        *[pltpu.VMEM((rows, blk, wide), F32)] * 2,
        *[pltpu.VMEM((2, fetch, blk, wide), F32)] * 4,
        *[pltpu.VMEM((rows, 3, blk, wide), BF16)] * 2,
        *[pltpu.VMEM((2 * fetch, 3, blk, wide), BF16)] * 2,
        *[pltpu.VMEM((3, wide, rows * blk), BF16)] * 2,
        *[pltpu.VMEM((5, rows * blk, wide), BF16)] * 2,
        *[pltpu.VMEM((2, 5, wide, wide), F32)] * 2,
        pltpu.VMEM((5, wide, wide), F32),
        pltpu.SemaphoreType.DMA((4,)),
        pltpu.SemaphoreType.DMA((2, 8)),
        pltpu.SemaphoreType.DMA((2, 8)),
    ]
    return pl.pallas_call(
        functools.partial(kernel, rows, gx_size, gy_size),
        out_shape=jax.ShapeDtypeStruct((coarse_inv.shape[0], 7 * AGG_DEV, blk, blk), F32),
        in_specs=[pl.BlockSpec(memory_space=pltpu.SMEM), hbm, hbm, hbm, hbm],
        out_specs=pl.BlockSpec(memory_space=pltpu.VMEM),
        scratch_shapes=scratch,
        compiler_params=pltpu.CompilerParams(
            collective_id=0, has_side_effects=True, vmem_limit_bytes=56 * 1024 * 1024
        ),
    )(idx, a_blocks, t_blocks, dinv, coarse_inv)


def solution(mesh):
    placed = (
        P(("gx", "gy"), None, None, None),
        P(),
        P(("gx", "gy"), None, None),
        P(),
        P(("gx", "gy"), None, None),
        P(("gx", "gy"), None, None),
    )
    return jax.shard_map(
        functools.partial(shards, mesh.shape["gx"], mesh.shape["gy"]),
        mesh=mesh,
        in_specs=placed,
        out_specs=P(("gx", "gy"), None, None, None),
        check_vma=False,
    )
```

time: 313 us -> 78.5 us (0.25); the launches traced: 309 us -> 78.3 us
  other arithmetic: 91.8 us -> 2.59 us
  local copies, waits for them, and re-layouts: 79.2 us -> 7.93 us
  matrix products: 67.9 us -> 0 us
  Pallas kernels: 0 us -> 67.7 us
  waiting for transfers between devices: 64.7 us -> 0 us
  starting transfers between devices: 4.19 us -> 0 us
    scatter-add x8 -> x0, other arithmetic: 83 us -> none  [accumulate(): return buffer.at[target_all, slot].add(contrib)]
    dot_general x27 -> x0, matrix products: 67.9 us -> none  [the longest x8 25.9 us: accumulate(): contrib = jnp.einsum('pba,nbc->pnac', p_row, grouped, precision=highest)]
    pallas_call x0 -> x1, Pallas kernels: none -> 67.7 us  [shards(): pl.pallas_call(functools.partial(kernel, rows, gx_size, gy_size), out_sha...]
    ppermute x6 -> x0, waiting for transfers between devices: 64.7 us -> none  [shifted(): return lax.ppermute(value, axis, pairs)]
    gather x19 -> x8, local copies, waits for them, and re-layouts: 33.7 us -> 3.38 us  [the longest x2 0.79 us: indices(): labels = t_agg[own]]
    transpose x17 -> x3, local copies, waits for them, and re-layouts: 22.9 us -> 0.28 us  [the longest x1 0.1 us: indices(): up_labels.T.reshape(-1)]
    while x32 -> x0, local copies, waits for them, and re-layouts: 8.93 us -> none
    concatenate x10 -> x0, other arithmetic: 5.53 us -> none  [the longest x1 3.85 us: shards(): p_extended = jnp.concatenate([p_lower, prolong, p_upper], axis=0)]
  transfers between devices with their start and end apart: 6 -> 0, of which waited for: 4 -> 0; matrix products, arithmetic and copies ran while one was open for 3% -> 0% of each run, Pallas kernels for 0% -> 0%
where the time goes in v1:
time: 78.5 us; the launch traced here: 78.3 us
  Pallas kernels  67.7 us (86%)
  local copies, waits for them, and re-layouts  7.93 us (10%)
  other arithmetic  2.59 us (3%)
    pallas_call x1, Pallas kernels, shards(): pl.pallas_call(functools.partial(kernel, rows, gx_size, gy_size), out_sha...  67.7 us
    unnamed x6, local copies, waits for them, and re-layouts  3.08 us

profile of v1, /device:TPU:29, one launch (start us, length us, event | category | flops | bytes accessed | tf_op | source)
XLA Modules:
  0.0 78.3 jit_solution(3799553393105338293)
XLA Ops:
  0.0 0.9 %constant_dynamic-slice_fusion = (s32[8,4]{0,1:T(4,128)S(1)}, s32[8,4]{0,1:T(4,128)S(1)}, s32[8,4]{0,1:T(4,128)S(1)}, s32[8,4]{0,1:T(4,128)S(1)}) fusion(s32[256,4]{0,1:T(4,128)} %param.7, s32[]{:T(128)S(6)} %select_n.129, s32[]{:T(128)S(6)} %select_n.124, s32[]{:T(128)S(6)} %select_n.112), kind=kLoop, calls=%fused_computation.58 | loop fusion | flops 96 | bytes 908 | tf_op jit(solution)/shard_map/dynamic_slice | solution.py:23
  0.9 0.1 fusion.3
  1.0 0.1 select_reduce_fusion
  1.1 0.1 select_reduce_fusion.4
  1.3 0.1 fusion.1
  1.4 0.1 fusion
  1.4 0.1 fusion.2
  1.5 0.1 select_reduce_fusion.1
  1.7 0.1 select_reduce_fusion.5
  1.8 0.1 select_reduce_fusion.3
  1.9 0.1 select_reduce_fusion.9
  2.0 0.1 select_reduce_fusion.8
  2.1 0.1 select_reduce_fusion.2
  2.2 0.1 select_reduce_fusion.7
  2.4 0.1 select_reduce_fusion.6
  2.7 0.7 gather_fusion
  3.5 0.1 copy.20
  3.5 0.1 reshape.83
  3.6 0.1 copy.21
  3.8 0.6 gather_fusion.3
  4.3 0.6 gather_fusion.1
  5.0 0.1 reshape.104
  5.1 0.1 reshape.120
  5.2 0.6 gather_fusion.4
  6.0 0.1 copy.24
  6.1 0.1 reshape.85
  6.1 0.7 gather_fusion.2
  6.8 0.1 reshape.103
  6.9 0.1 copy.22
  7.1 0.6 concatenate.3.idx
  7.7 67.7 %shard_map.64 = f32[2,14,128,128]{3,2,1,0:T(8,128)} custom-call(s32[80]{0:T(128)} %concatenate.3.idx, f32[8,4,128,128]{3,2,1,0:T(8,128)} %a_hbm.1, f32[8,128,128]{2,1,0:T(8,128)} %t_hbm.1, f32[8,128,128]{2,1,0:T(8,128)} %d_hbm.1, f32[2,128,128]{2,1,0:T(8,128)} %c_hbm.1), custom_call_target="tpu_custom_call" | custom-call | tf_op jit(solution)/shard_map/pallas_call | solution.py:336
  75.4 2.9 %copy.26 = f32[2,14,128,128]{3,2,1,0:T(8,128)} copy(f32[2,14,128,128]{3,2,1,0:T(8,128)} %shard_map.64) | data formatting | bytes 3670016
  (26 shorter events, 0.7 us)
Async XLA Ops:
  0.0 2.6 %copy-start = (s32[256]{0:T(256)S(1)}, s32[256]{0:T(256)}, u32[]{:S(2)}) copy-start(s32[256]{0:T(256)} %param.9) | copy-start | bytes 3076
  2.7 1.0 %copy-start.1 = (s32[256,4]{0,1:T(4,128)S(1)}, s32[256,4]{0,1:T(4,128)}, u32[]{:S(2)}) copy-start(s32[256,4]{0,1:T(4,128)} %param.7) | copy-start | bytes 12292

commit v2 on v1

--- a/solution.py
+++ b/solution.py
@@ -19,48 +19,52 @@
 FINAL_ORDER = (1, 5, 3, 2, 0, 4, 6)
 
 
-def read_list(a_cols, slab, side, rows):
-    block_cols = lax.dynamic_slice_in_dim(a_cols, slab * rows, rows, 0)[:, 2 + side]
-    offsets = block_cols % rows
-    counter = jnp.arange(rows, dtype=jnp.int32)
-    is_read = jnp.any(offsets[:, None] == counter[None, :], axis=0).astype(jnp.int32)
-    ranks = jnp.sum(jnp.where(counter[None, :] < counter[:, None], is_read[None, :], 0), axis=1)
-    places = jnp.arange(rows // 2, dtype=jnp.int32)
-    matched = (is_read[:, None] == 1) & (ranks[:, None] == places[None, :])
-    return jnp.sum(jnp.where(matched, counter[:, None], 0), axis=0)
-
-
-def indices(a_cols, t_agg, device, devices, rows):
-    previous = (device + devices - 1) % devices
-    following = (device + 1) % devices
-    own = lax.dynamic_slice_in_dim(a_cols, device * rows, rows, 0)
-    offsets = own % rows
-    lower_list = read_list(a_cols, device, 0, rows)
-    upper_list = read_list(a_cols, device, 1, rows)
-    to_upper = read_list(a_cols, following, 0, rows)
-    to_lower = read_list(a_cols, previous, 1, rows)
-    places = jnp.arange(rows // 2, dtype=jnp.int32)
-
-    def rank(entries, offs):
-        return jnp.sum(jnp.where(entries[None, :] == offs[:, None], places[None, :], 0), axis=1)
-
-    labels = t_agg[own]
-    low_cols = a_cols[previous * rows + lower_list][:, 2:4]
-    up_cols = a_cols[following * rows + upper_list][:, 2:4]
-    low_labels = t_agg[low_cols]
-    up_labels = t_agg[up_cols]
-    return jnp.concatenate(
-        [
-            offsets[:, 1],
-            rank(lower_list, offsets[:, 2]),
-            rank(upper_list, offsets[:, 3]),
-            labels.T.reshape(-1),
-            to_upper,
-            to_lower,
-            low_labels.T.reshape(-1),
-            up_labels.T.reshape(-1),
-        ]
-    ).astype(jnp.int32)
+def read_lists(cols, labels, idx, rows, me, following, previous):
+    fetch = rows // 2
+
+    def offset(slab, row, k):
+        return lax.rem(cols[(slab * rows + row) * 4 + k], rows)
+
+    def one(value):
+        return value.astype(jnp.int32)
+
+    def read_list(slab, side):
+        offs = [offset(slab, r, 2 + side) for r in range(rows)]
+        read = [functools.reduce(jnp.maximum, [one(o == c) for o in offs]) for c in range(rows)]
+        picks = [0] * fetch
+        before = 0
+        for c in range(rows):
+            for j in range(max(0, c - fetch), min(c, fetch - 1) + 1):
+                picks[j] = picks[j] + jnp.where(before == j, c * read[c], 0)
+            before = before + read[c]
+        return offs, read, picks
+
+    base_to = 7 * rows
+    for side, slab in ((0, following), (1, previous)):
+        picks = read_list(slab, side)[2]
+        for j in range(fetch):
+            idx[base_to + side * fetch + j] = picks[j]
+
+    def rest():
+        for side, slab in ((0, previous), (1, following)):
+            offs, read, picks = read_list(me, side)
+            ranks = [0]
+            for c in range(rows - 1):
+                ranks.append(ranks[-1] + read[c])
+            for r in range(rows):
+                idx[(1 + side) * rows + r] = functools.reduce(
+                    jnp.add, [jnp.where(offs[r] == c, ranks[c], 0) for c in range(1, rows)]
+                )
+            for j in range(fetch):
+                for far in range(2):
+                    entry = cols[(slab * rows + picks[j]) * 4 + 2 + far]
+                    idx[base_to + 2 * fetch + (side * 2 + far) * fetch + j] = labels[entry]
+        for r in range(rows):
+            idx[r] = offset(me, r, 1)
+            for k in range(4):
+                idx[(3 + k) * rows + r] = labels[cols[(me * rows + r) * 4 + k]]
+
+    return rest
 
 
 def split(x):
@@ -77,13 +81,14 @@
 
 def kernel(
     rows, gx_size, gy_size,
-    idx, a_hbm, t_hbm, d_hbm, c_hbm, out,
+    cols_s, labels_s, a_hbm, t_hbm, d_hbm, c_hbm, out,
+    idx, out_v,
     a_v, t_v, d_v, c_v,
     ah, al, bh, bl, th, tl,
     t_send, t_recv, own_c, far_c, po_send, po_recv, pf_send, pf_recv,
     pdh, pdl, ndh, ndl, pth, ptl, aph, apl,
     g_send, g_recv, g_own,
-    load_sem, send_sem, recv_sem,
+    load_sem, send_sem, recv_sem, out_sem,
 ):
     fetch = rows // 2
     blk = t_v.shape[-1]
@@ -125,6 +130,7 @@
     base_to = 7 * rows
     base_near = base_to + 2 * fetch
 
+    rest = read_lists(cols_s, labels_s, idx, rows, me, following, previous)
     loads[0].wait()
     for side in range(2):
         for j in range(fetch):
@@ -132,6 +138,7 @@
     pl.semaphore_wait(barrier, 2)
     t_copies = [send(t_send.at[side], t_recv.at[side], side, 0) for side in range(2)]
 
+    rest()
     loads[1].wait()
     loads[2].wait()
 
@@ -282,6 +289,7 @@
 
     loads[3].wait()
     inverses = [split(c_v[a]) for a in range(AGG_DEV)]
+    stores = []
     for j in FINAL_ORDER:
         if j <= 4:
             g_copies[0, j].wait_recv()
@@ -299,21 +307,28 @@
             h, l = split(functools.reduce(jnp.add, terms))
             result = dot3(inverses[a][0], inverses[a][1], h, l)
             for v in range(AGG_DEV):
-                out[a, AGG_DEV * j + v] = result[:, v * blk:(v + 1) * blk]
+                out_v[a, AGG_DEV * j + v] = result[:, v * blk:(v + 1) * blk]
+            slots = pl.ds(AGG_DEV * j, AGG_DEV)
+            store = pltpu.make_async_copy(out_v.at[a, slots], out.at[a, slots], out_sem.at[a, j])
+            store.start()
+            stores.append(store)
 
     for copy in [*t_copies, *po_copies, *pf_copies, *g_copies.values()]:
         copy.wait_send()
+    for store in stores:
+        store.wait()
 
 
 def shards(gx_size, gy_size, a_blocks, a_cols, t_blocks, t_agg, dinv, coarse_inv):
-    devices = gx_size * gy_size
-    device = lax.axis_index(("gx", "gy"))
     rows, blk = t_blocks.shape[0], t_blocks.shape[1]
     fetch = rows // 2
     wide = AGG_DEV * blk
-    idx = indices(a_cols, t_agg, device, devices, rows)
+    shape = (coarse_inv.shape[0], 7 * AGG_DEV, blk, blk)
     hbm = pl.BlockSpec(memory_space=pl.ANY)
+    smem = pl.BlockSpec(memory_space=pltpu.SMEM)
     scratch = [
+        pltpu.SMEM((7 * rows + 6 * fetch,), jnp.int32),
+        pltpu.VMEM(shape, F32),
         pltpu.VMEM(a_blocks.shape, F32),
         pltpu.VMEM(t_blocks.shape, F32),
         pltpu.VMEM(dinv.shape, F32),
@@ -332,17 +347,18 @@
         pltpu.SemaphoreType.DMA((4,)),
         pltpu.SemaphoreType.DMA((2, 8)),
         pltpu.SemaphoreType.DMA((2, 8)),
+        pltpu.SemaphoreType.DMA((AGG_DEV, 7)),
     ]
     return pl.pallas_call(
         functools.partial(kernel, rows, gx_size, gy_size),
-        out_shape=jax.ShapeDtypeStruct((coarse_inv.shape[0], 7 * AGG_DEV, blk, blk), F32),
-        in_specs=[pl.BlockSpec(memory_space=pltpu.SMEM), hbm, hbm, hbm, hbm],
-        out_specs=pl.BlockSpec(memory_space=pltpu.VMEM),
+        out_shape=jax.ShapeDtypeStruct(shape, F32),
+        in_specs=[smem, smem, hbm, hbm, hbm, hbm],
+        out_specs=hbm,
         scratch_shapes=scratch,
         compiler_params=pltpu.CompilerParams(
             collective_id=0, has_side_effects=True, vmem_limit_bytes=56 * 1024 * 1024
         ),
-    )(idx, a_blocks, t_blocks, dinv, coarse_inv)
+    )(a_cols.reshape(-1), t_agg, a_blocks, t_blocks, dinv, coarse_inv)
 
 
 def solution(mesh):

time: 78.5 us -> 72 us (0.917)
  local copies, waits for them, and re-layouts: 7.93 us -> 4.46 us
  other arithmetic: 2.59 us -> 0 us
    gather x8 -> x0, local copies, waits for them, and re-layouts: 3.38 us -> none  [the longest x2 0.79 us: indices(): labels = t_agg[own]]
    reduce_sum x10 -> x0, other arithmetic: 1.11 us -> none  [the longest x4 0.48 us: read_list(): return jnp.sum(jnp.where(matched, counter[:, None], 0), axis=0)]
    dynamic_slice x1 -> x0, other arithmetic: 0.86 us -> none  [read_list(): lax.dynamic_slice_in_dim(a_cols, slab * rows, rows, 0)[:, 2 + side]]
    unnamed x6 -> x2, local copies, waits for them, and re-layouts: 3.08 us -> 3.74 us
where the time goes in v2:
time: 72 us; the launch traced here: 71.8 us
  Pallas kernels  67.3 us (93%)
  local copies, waits for them, and re-layouts  4.46 us (6%)
    pallas_call x1, Pallas kernels, shards(): pl.pallas_call(functools.partial(kernel, rows, gx_size, gy_size), out_sha...  67.3 us
    unnamed x2, local copies, waits for them, and re-layouts  3.74 us

profile of v2, /device:TPU:29, one launch (start us, length us, event | category | flops | bytes accessed | tf_op | source)
XLA Modules:
  0.0 71.8 jit_solution(3315002557547069423)
XLA Ops:
  0.0 0.8 %copy.7 = s32[256,4]{1,0:T(8,128)S(1)} copy(s32[256,4]{0,1:T(4,128)} %param.7) | data formatting | bytes 8192 | tf_op args[1]
  0.8 0.7 reshape.3.cols_s
  1.5 67.3 %shard_map.64 = f32[2,14,128,128]{3,2,1,0:T(8,128)} custom-call(s32[1024]{0:T(1024)} %reshape.3.cols_s, s32[256]{0:T(256)} %labels_s.1, f32[8,4,128,128]{3,2,1,0:T(8,128)} %a_hbm.1, f32[8,128,128]{2,1,0:T(8,128)} %t_hbm.1, f32[8,128,128]{2,1,0:T(8,128)} %d_hbm.1, f32[2,128,128]{2,1,0:T(8,128)} %c_hbm.1), custom_call_target="tpu_custom_call" | custom-call | tf_op jit(solution)/shard_map/pallas_call | solution.py:352
  68.9 2.9 %copy.9 = f32[2,14,128,128]{3,2,1,0:T(8,128)} copy(f32[2,14,128,128]{3,2,1,0:T(8,128)} %shard_map.64) | data formatting | bytes 3670016
